TPU v7x, 32 devices: a whole 2x2x4 slice. The times are simulated.
32 devices in a mesh: scene: 2 (over y), row: 16 (over z, x, core).
Axes of the slice: x: 2, y: 2, z: 4, core: 2. Of those that a mesh axis runs over, the one named last changes fastest.
Arguments:
- adjoint_seed: float32 [64, 8192], P(None, ('scene', 'row')), parts along dimension 1, may hold values from -1 to 1
- radiosity: bfloat16 [64, 8192], P(None, ('scene', 'row')), parts along dimension 1, may hold values from -6 to 6
- emission: bfloat16 [64, 8192], P(None, ('scene', 'row')), parts along dimension 1, may hold values from -6 to 6
- reflectance: float32 [8192], P(('scene', 'row')), parts along dimension 0, may hold values from 0.2 to 0.9
- area: float32 [8192], P(('scene', 'row')), parts along dimension 0, may hold values from 0.5 to 4
- position: float32 [3, 8192], P(None, ('scene', 'row')), parts along dimension 1, may hold values from -4 to 4
- visibility: int32 [64, 32], P(('scene', 'row')), parts along dimension 0, may hold values from -2147483648 to 2147483647, as said below
Outputs:
- adjoint_field: float32 [64, 8192], P(None, ('scene', 'row')), parts along dimension 1
- reflect_grad: float32 [8192], P(('scene', 'row')), parts along dimension 0
There are 2 independent parts, one for each index of `scene`. A program takes and returns all parts, laid end to end along the dimension named above; each array names one. Nothing has to cross between parts.
Inputs may be any that keep to these rules, and one draw needn't show every extreme that they name: visibility is symmetric: visibility[I, J] equals visibility[J, I]; its words use all 32 bits.
All inputs are finite; a program needn't handle non-finite values.
Results may differ from a plain program's by a relative error of at most 0.0026.
Values may be sent and summed in bfloat16 or wider, within the bound.
No kernel may reach another device: no remote copies, remote signals or barrier semaphores. Data moves between devices by JAX's collectives and lax.ppermute only.
A program may use at most 64 MiB of HBM per device.

v0:
```python
import functools
import math

import jax
import jax.numpy as jnp
from jax import lax
from jax.experimental import pallas as pl
from jax.experimental.pallas import tpu as pltpu
from jax.sharding import PartitionSpec as P

TILE = 128
SWEEPS = 2
GROUP = 16
EXTRA = 16
DIRECT = 16
VMEM_BYTES = 48 * 1024 * 1024


def position_rows(pos):
    high = pos.astype(jnp.bfloat16).astype(jnp.float32)
    rest = pos - high
    middle = rest.astype(jnp.bfloat16).astype(jnp.float32)
    return high, middle, rest - middle


def spread_rows(pos_ref, spread):
    for coord in range(3):
        for block in range(spread.shape[1]):
            line = pos_ref[coord : coord + 1, block * TILE : (block + 1) * TILE]
            spread[coord, block] = jnp.transpose(jnp.broadcast_to(line, (TILE, TILE)))


def inverse_square(spread, lines, own_block, rows, other_block):
    lanes = slice(other_block * TILE, (other_block + 1) * TILE)
    total = 1.0
    for coord in range(3):
        delta = spread[coord, own_block, rows, :] - lines[coord][:, lanes]
        total = total + delta * delta
    return 1.0 / total


def form_part(me, part, at, words_ref, lines, spread, kernel_ref):
    blocks = spread.shape[1]
    lane = lax.broadcasted_iota(jnp.int32, (GROUP, TILE), 1)
    for own_block in range(blocks):
        row_block = me * blocks + own_block
        for other_block in range(blocks):
            col_block = part * blocks + other_block
            word = words_ref[own_block, col_block]
            direct = row_block < col_block
            for group in range(TILE // GROUP):
                rows = slice(group * GROUP, (group + 1) * GROUP)
                bit = jnp.where(direct, 8 * (group // 2) + lane // 16, 8 * (lane // 32) + group)
                seen = (jnp.right_shift(word, bit) & 1) != 0
                value = inverse_square(spread, lines, own_block, rows, other_block)
                value = jnp.where(seen, value, 0.0).astype(jnp.bfloat16)
                kernel_ref[
                    at,
                    own_block * TILE + group * GROUP : own_block * TILE + (group + 1) * GROUP,
                    other_block * TILE : (other_block + 1) * TILE,
                ] = value


def form_diagonal(me, at, words_ref, lines, spread, kernel_ref):
    blocks = spread.shape[1]
    lane = lax.broadcasted_iota(jnp.int32, (TILE, TILE), 1)
    row = lax.broadcasted_iota(jnp.int32, (TILE, TILE), 0)
    low, high = jnp.minimum(row, lane), jnp.maximum(row, lane)
    bit = 8 * (low // 32) + high // 16
    for block in range(blocks):
        word = words_ref[block, me * blocks + block]
        seen = (jnp.right_shift(word, bit) & 1) != 0
        value = inverse_square(spread, lines, block, slice(0, TILE), block)
        value = jnp.where(seen, value, 0.0).astype(jnp.bfloat16)
        span = slice(block * TILE, (block + 1) * TILE)
        kernel_ref[at, span, span] = value


def times_transpose(values, kernel):
    return lax.dot_general(
        values, kernel, (((1,), (1,)), ((), ())), preferred_element_type=jnp.float32
    )


def prepare(pos_ref, seed_ref, reflectance_ref, out_ref, rows):
    rhs_count = seed_ref.shape[0]
    rows[...] = jnp.zeros_like(rows)
    for term, value in enumerate(position_rows(pos_ref[...])):
        rows[3 * term : 3 * term + 3, :] = value
    scaled = (reflectance_ref[...] * seed_ref[...]).astype(jnp.bfloat16)
    extra = rows[...].astype(jnp.bfloat16)
    for copy in range(out_ref.shape[0]):
        out_ref[copy, :rhs_count] = scaled
        out_ref[copy, rhs_count:] = extra


def lines_of(extra):
    extra = extra.astype(jnp.float32)
    return [
        extra[coord : coord + 1] + extra[3 + coord : 4 + coord] + extra[6 + coord : 7 + coord]
        for coord in range(3)
    ]


def first_sweep(
    scale,
    me_ref,
    words_ref,
    own_pos_ref,
    packed_ref,
    seed_ref,
    area_ref,
    reflectance_ref,
    kernel_ref,
    scaled_ref,
    spread,
    total,
):
    step = pl.program_id(0)
    chunk = packed_ref.shape[0]
    rhs_count = seed_ref.shape[0]
    me = me_ref[0]

    @pl.when(step == 0)
    def _():
        spread_rows(own_pos_ref, spread)
        total[...] = jnp.zeros_like(total)

    def form(at, carry):
        lines = lines_of(packed_ref[at, rhs_count:])
        form_part(me, step * chunk + at, at, words_ref, lines, spread, kernel_ref)
        return carry

    lax.fori_loop(0, chunk, form, 0)

    @pl.when((me >= step * chunk) & (me < (step + 1) * chunk))
    def _():
        lines = [own_pos_ref[coord : coord + 1, :] for coord in range(3)]
        form_diagonal(me, me - step * chunk, words_ref, lines, spread, kernel_ref)

    held = total[...]
    for at in range(chunk):
        held += times_transpose(packed_ref[at, :rhs_count], kernel_ref[at])
    total[...] = held

    @pl.when(step == pl.num_programs(0) - 1)
    def _():
        adjoint = seed_ref[...] + (area_ref[...] * scale) * total[...]
        scaled_ref[...] = (reflectance_ref[...] * adjoint).astype(jnp.bfloat16)


def finish(
    scale, total, seed_ref, area_ref, reflectance_ref, radiosity_ref, emission_ref, adjoint_ref, grad_ref
):
    adjoint = seed_ref[...] + (area_ref[...] * scale) * total
    adjoint_ref[...] = adjoint
    change = radiosity_ref[...].astype(jnp.float32) - emission_ref[...].astype(jnp.float32)
    grad_ref[...] = jnp.sum(adjoint * change, axis=0, keepdims=True) / reflectance_ref[...]


def last_sweep(scale, kernel_ref, every_ref, *rest):
    step = pl.program_id(0)
    total = rest[-1]

    @pl.when(step == 0)
    def _():
        total[...] = jnp.zeros_like(total)

    held = total[...]
    for at in range(every_ref.shape[0]):
        held += times_transpose(every_ref[at], kernel_ref[at])
    total[...] = held

    @pl.when(step == pl.num_programs(0) - 1)
    def _():
        finish(scale, total[...], *rest[:-1])


def last_sweep_direct(scale, pieces, me_ref, kernel_ref, *rest):
    me = me_ref[0]
    held = times_transpose(rest[0][...], kernel_ref[me])
    for step in range(1, pieces):
        held += times_transpose(rest[step][...], kernel_ref[jnp.bitwise_xor(me, step)])
    finish(scale, held, *rest[pieces:])


def whole(shape):
    return pl.BlockSpec(shape, lambda step: (0,) * len(shape))


def parts(chunk, shape):
    return pl.BlockSpec((chunk,) + shape, lambda step: (step,) + (0,) * len(shape))


def on_device(adjoint_seed, radiosity, emission, reflectance, area, position, visibility):
    rhs_count, own_width = adjoint_seed.shape
    devices = lax.axis_size("row")
    my_index = lax.axis_index("row").astype(jnp.int32).reshape(1)
    local_blocks = own_width // TILE
    scale = 1.0 / math.sqrt(own_width * devices)
    chunk = math.gcd(devices, 16)
    direct = devices <= DIRECT and devices & (devices - 1) == 0
    area = area.reshape(1, own_width)
    reflectance = reflectance.reshape(1, own_width)
    smem = pl.BlockSpec(memory_space=pltpu.SMEM)
    vmem = pl.BlockSpec(memory_space=pltpu.VMEM)
    params = pltpu.CompilerParams(
        dimension_semantics=("arbitrary",), vmem_limit_bytes=VMEM_BYTES
    )
    packed_rows = rhs_count + EXTRA

    packed = pl.pallas_call(
        prepare,
        in_specs=[vmem] * 3,
        out_specs=vmem,
        out_shape=jax.ShapeDtypeStruct(
            (devices if direct else 1, packed_rows, own_width), jnp.bfloat16
        ),
        scratch_shapes=[pltpu.VMEM((EXTRA, own_width), jnp.float32)],
        name="prepare",
    )(position, adjoint_seed, reflectance)
    if direct:
        packed = lax.all_to_all(packed, "row", 0, 0)
    else:
        packed = lax.all_gather(packed[0], "row")
    kernel, scaled = pl.pallas_call(
        functools.partial(first_sweep, scale),
        grid=(devices // chunk,),
        in_specs=[
            smem,
            smem,
            whole((3, own_width)),
            parts(chunk, (packed_rows, own_width)),
            whole((rhs_count, own_width)),
            whole((1, own_width)),
            whole((1, own_width)),
        ],
        out_specs=[parts(chunk, (own_width, own_width)), whole((rhs_count, own_width))],
        out_shape=[
            jax.ShapeDtypeStruct((devices, own_width, own_width), jnp.bfloat16),
            jax.ShapeDtypeStruct((rhs_count, own_width), jnp.bfloat16),
        ],
        scratch_shapes=[
            pltpu.VMEM((3, local_blocks, TILE, TILE), jnp.float32),
            pltpu.VMEM((rhs_count, own_width), jnp.float32),
        ],
        compiler_params=params,
        name="first_sweep",
    )(my_index, visibility, position, packed, adjoint_seed, area, reflectance)

    out_shape = [
        jax.ShapeDtypeStruct((rhs_count, own_width), jnp.float32),
        jax.ShapeDtypeStruct((1, own_width), jnp.float32),
    ]
    own = (adjoint_seed, area, reflectance, radiosity, emission)
    if direct:
        pieces = [scaled]
        for step in range(1, devices):
            pairs = [(device, device ^ step) for device in range(devices)]
            pieces.append(lax.ppermute(scaled, "row", pairs))
        adjoint, grad = pl.pallas_call(
            functools.partial(last_sweep_direct, scale, devices),
            in_specs=[smem] + [vmem] * (devices + 6),
            out_specs=[vmem, vmem],
            out_shape=out_shape,
            compiler_params=pltpu.CompilerParams(vmem_limit_bytes=VMEM_BYTES),
            name="last_sweep",
        )(my_index, kernel, *pieces, *own)
        return adjoint, grad.reshape(own_width)

    every = lax.all_gather(scaled, "row")
    adjoint, grad = pl.pallas_call(
        functools.partial(last_sweep, scale),
        grid=(devices // chunk,),
        in_specs=[
            parts(chunk, (own_width, own_width)),
            parts(chunk, (rhs_count, own_width)),
            whole((rhs_count, own_width)),
            whole((1, own_width)),
            whole((1, own_width)),
            whole((rhs_count, own_width)),
            whole((rhs_count, own_width)),
        ],
        out_specs=[whole((rhs_count, own_width)), whole((1, own_width))],
        out_shape=out_shape,
        scratch_shapes=[pltpu.VMEM((rhs_count, own_width), jnp.float32)],
        compiler_params=params,
        name="last_sweep",
    )(kernel, every, *own)
    return adjoint, grad.reshape(own_width)


def solution(mesh):
    placed = (
        P(None, ("scene", "row")),
        P(None, ("scene", "row")),
        P(None, ("scene", "row")),
        P(("scene", "row")),
        P(("scene", "row")),
        P(None, ("scene", "row")),
        P(("scene", "row"), None),
    )
    return jax.shard_map(
        on_device,
        mesh=mesh,
        in_specs=placed,
        out_specs=(P(None, ("scene", "row")), P(("scene", "row"))),
        check_vma=False,
    )
```

profile of v0, /device:TPU:0, one launch (start us, length us, event | category | flops | bytes accessed | tf_op | source)
XLA Modules:
  0.0 59.0 jit_solution(8777192239714298761)
XLA Ops:
  0.6 0.0 copy-start.1
  0.6 0.0 copy-start.6
  0.7 0.0 copy-start.3
  0.7 0.0 copy-start.2
  0.7 1.8 %prepare.1 = bf16[16,80,256]{2,1,0:T(8,128)(2,1)} custom-call(f32[3,256]{1,0:T(4,128)} %own_pos_ref.1, f32[64,256]{1,0:T(8,128)} %rest_16_.1, f32[1,256]{1,0:T(1,128)} %bitcast.4), custom_call_target="tpu_custom_call" | custom-call | tf_op jit(solution)/shard_map/prepare/pallas_call | solution.py:212
  2.5 7.4 %all-to-all-start = ((bf16[16,80,256]{2,1,0:T(8,128)(2,1)}), bf16[16,80,256]{2,1,0:T(8,128)(2,1)S(1)}, u32[]{:S(2)}, u32[]{:S(2)}) async-start(bf16[16,80,256]{2,1,0:T(8,128)(2,1)} %prepare.1), calls=%async_computation | async-start | bytes 1310720 | tf_op jit(solution)/shard_map/all_to_all | solution.py:223
  9.8 16.6 %all-to-all-done.packed_ref = bf16[16,80,256]{2,1,0:T(8,128)(2,1)S(1)} async-done(((bf16[16,80,256]{2,1,0:T(8,128)(2,1)}), bf16[16,80,256]{2,1,0:T(8,128)(2,1)S(1)}, u32[]{:S(2)}, u32[]{:S(2)}) %all-to-all-start) | async-done | bytes 655392 | tf_op jit(solution)/shard_map/all_to_all | solution.py:223
  26.4 0.0 copy-start
  26.4 0.8 %copy-done = f32[64,256]{1,0:T(8,128)S(1)} copy-done((f32[64,256]{1,0:T(8,128)S(1)}, f32[64,256]{1,0:T(8,128)}, u32[]{:S(2)}) %copy-start) | copy-done | bytes 65560
  27.3 0.0 copy-start.4
  27.3 0.7 %copy-done.4 = f32[3,256]{1,0:T(4,128)S(1)} copy-done((f32[3,256]{1,0:T(4,128)S(1)}, f32[3,256]{1,0:T(4,128)}, u32[]{:S(2)}) %copy-start.4) | copy-done | bytes 3096
  27.9 0.0 copy-start.5
  28.0 0.7 %copy-done.5 = f32[256]{0:T(256)S(1)} copy-done((f32[256]{0:T(256)S(1)}, f32[256]{0:T(256)}, u32[]{:S(2)}) %copy-start.5) | copy-done | bytes 1048
  28.6 0.0 copy-start.7
  28.6 0.7 %copy-done.7 = f32[256]{0:T(256)S(1)} copy-done((f32[256]{0:T(256)S(1)}, f32[256]{0:T(256)}, u32[]{:S(2)}) %copy-start.7) | copy-done | bytes 1048
  29.3 0.0 copy-start.8
  29.3 0.7 %copy-done.8 = s32[2,32]{1,0:T(2,128)S(1)} copy-done((s32[2,32]{1,0:T(2,128)S(1)}, s32[2,32]{1,0:T(2,128)}, u32[]{:S(2)}) %copy-start.8) | copy-done | bytes 280
  30.0 3.8 %first_sweep.1 = (bf16[16,256,256]{2,1,0:T(8,128)(2,1)S(1)}, bf16[64,256]{1,0:T(8,128)(2,1)S(1)}) custom-call(s32[1]{0:T(128)} %bitcast.me_ref, s32[2,32]{1,0:T(2,128)S(1)} %copy-done.8, f32[3,256]{1,0:T(4,128)S(1)} %copy-done.4, bf16[16,80,256]{2,1,0:T(8,128)(2,1)S(1)} %all-to-all-done.packed_ref, f32[64,256]{1,0:T(8,128)S(1)} %copy-done, ...), custom_call_target="tpu_custom_call" | custom-call | tf_op jit(solution)/shard_map/first_sweep/pallas_call | solution.py:226
  33.8 3.4 %collective-permute-start.14 = (bf16[64,256]{1,0:T(8,128)(2,1)S(1)}, bf16[64,256]{1,0:T(8,128)(2,1)S(1)}, u32[]{:S(2)}, u32[]{:S(2)}) collective-permute-start(bf16[64,256]{1,0:T(8,128)(2,1)S(1)} %get-tuple-element.7.rest_0_), channel_id=1, source_target_pairs={{0,15},{1,14},{2,13},{3,12},{4,11},{5,10},{6,9},{7,8},{8,7},{9,6},... | collective-permute-start | bytes 98312 | tf_op jit(solution)/shard_map/ppermute | solution.py:260
  37.2 1.1 %collective-permute-start.13 = (bf16[64,256]{1,0:T(8,128)(2,1)S(1)}, bf16[64,256]{1,0:T(8,128)(2,1)S(1)}, u32[]{:S(2)}, u32[]{:S(2)}) collective-permute-start(bf16[64,256]{1,0:T(8,128)(2,1)S(1)} %get-tuple-element.7.rest_0_), channel_id=1, source_target_pairs={{0,14},{1,15},{2,12},{3,13},{4,10},{5,11},{6,8},{7,9},{8,6},{9,7},... | collective-permute-start | bytes 98312 | tf_op jit(solution)/shard_map/ppermute | solution.py:260
  38.3 1.4 %collective-permute-start.12 = (bf16[64,256]{1,0:T(8,128)(2,1)S(1)}, bf16[64,256]{1,0:T(8,128)(2,1)S(1)}, u32[]{:S(2)}, u32[]{:S(2)}) collective-permute-start(bf16[64,256]{1,0:T(8,128)(2,1)S(1)} %get-tuple-element.7.rest_0_), channel_id=1, source_target_pairs={{0,13},{1,12},{2,15},{3,14},{4,9},{5,8},{6,11},{7,10},{8,5},{9,4},... | collective-permute-start | bytes 98312 | tf_op jit(solution)/shard_map/ppermute | solution.py:260
  39.7 2.2 %collective-permute-start.11 = (bf16[64,256]{1,0:T(8,128)(2,1)S(1)}, bf16[64,256]{1,0:T(8,128)(2,1)S(1)}, u32[]{:S(2)}, u32[]{:S(2)}) collective-permute-start(bf16[64,256]{1,0:T(8,128)(2,1)S(1)} %get-tuple-element.7.rest_0_), channel_id=1, source_target_pairs={{0,12},{1,13},{2,14},{3,15},{4,8},{5,9},{6,10},{7,11},{8,4},{9,5},... | collective-permute-start | bytes 98312 | tf_op jit(solution)/shard_map/ppermute | solution.py:260
  41.9 0.0 collective-permute-start.10
  41.9 0.0 collective-permute-done.14.rest_15_
  41.9 3.5 %collective-permute-start.9 = (bf16[64,256]{1,0:T(8,128)(2,1)S(1)}, bf16[64,256]{1,0:T(8,128)(2,1)S(1)}, u32[]{:S(2)}, u32[]{:S(2)}) collective-permute-start(bf16[64,256]{1,0:T(8,128)(2,1)S(1)} %get-tuple-element.7.rest_0_), channel_id=1, source_target_pairs={{0,10},{1,11},{2,8},{3,9},{4,14},{5,15},{6,12},{7,13},{8,2},{9,3},... | collective-permute-start | bytes 98312 | tf_op jit(solution)/shard_map/ppermute | solution.py:260
  45.4 0.0 collective-permute-done.13.rest_14_
  45.4 0.0 collective-permute-start.8
  45.4 0.0 collective-permute-done.12.rest_13_
  45.4 2.7 %collective-permute-start.7 = (bf16[64,256]{1,0:T(8,128)(2,1)S(1)}, bf16[64,256]{1,0:T(8,128)(2,1)S(1)}, u32[]{:S(2)}, u32[]{:S(2)}) collective-permute-start(bf16[64,256]{1,0:T(8,128)(2,1)S(1)} %get-tuple-element.7.rest_0_), channel_id=1, source_target_pairs={{0,8},{1,9},{2,10},{3,11},{4,12},{5,13},{6,14},{7,15},{8,0},{9,1},... | collective-permute-start | bytes 98312 | tf_op jit(solution)/shard_map/ppermute | solution.py:260
  48.1 0.0 collective-permute-done.11.rest_12_
  48.1 1.3 %collective-permute-start.6 = (bf16[64,256]{1,0:T(8,128)(2,1)S(1)}, bf16[64,256]{1,0:T(8,128)(2,1)S(1)}, u32[]{:S(2)}, u32[]{:S(2)}) collective-permute-start(bf16[64,256]{1,0:T(8,128)(2,1)S(1)} %get-tuple-element.7.rest_0_), channel_id=1, source_target_pairs={{0,7},{1,6},{2,5},{3,4},{4,3},{5,2},{6,1},{7,0},{8,15},{9,14},{10,... | collective-permute-start | bytes 98312 | tf_op jit(solution)/shard_map/ppermute | solution.py:260
  49.4 0.0 collective-permute-done.10.rest_11_
  49.4 1.3 %collective-permute-start.5 = (bf16[64,256]{1,0:T(8,128)(2,1)S(1)}, bf16[64,256]{1,0:T(8,128)(2,1)S(1)}, u32[]{:S(2)}, u32[]{:S(2)}) collective-permute-start(bf16[64,256]{1,0:T(8,128)(2,1)S(1)} %get-tuple-element.7.rest_0_), channel_id=1, source_target_pairs={{0,6},{1,7},{2,4},{3,5},{4,2},{5,3},{6,0},{7,1},{8,14},{9,15},{10,... | collective-permute-start | bytes 98312 | tf_op jit(solution)/shard_map/ppermute | solution.py:260
  50.7 0.0 collective-permute-done.9.rest_10_
  50.7 0.2 collective-permute-start.4
  50.9 0.0 collective-permute-done.8.rest_9_
  50.9 1.6 %collective-permute-start.3 = (bf16[64,256]{1,0:T(8,128)(2,1)S(1)}, bf16[64,256]{1,0:T(8,128)(2,1)S(1)}, u32[]{:S(2)}, u32[]{:S(2)}) collective-permute-start(bf16[64,256]{1,0:T(8,128)(2,1)S(1)} %get-tuple-element.7.rest_0_), channel_id=1, source_target_pairs={{0,4},{1,5},{2,6},{3,7},{4,0},{5,1},{6,2},{7,3},{8,12},{9,13},{10,... | collective-permute-start | bytes 98312 | tf_op jit(solution)/shard_map/ppermute | solution.py:260
  52.5 0.0 collective-permute-done.7.rest_8_
  52.5 1.1 %collective-permute-start.2 = (bf16[64,256]{1,0:T(8,128)(2,1)S(1)}, bf16[64,256]{1,0:T(8,128)(2,1)S(1)}, u32[]{:S(2)}, u32[]{:S(2)}) collective-permute-start(bf16[64,256]{1,0:T(8,128)(2,1)S(1)} %get-tuple-element.7.rest_0_), channel_id=1, source_target_pairs={{0,3},{1,2},{2,1},{3,0},{4,7},{5,6},{6,5},{7,4},{8,11},{9,10},{10,... | collective-permute-start | bytes 98312 | tf_op jit(solution)/shard_map/ppermute | solution.py:260
  53.6 0.0 collective-permute-done.6.rest_7_
  53.6 0.6 collective-permute-start.1
  54.2 0.0 collective-permute-done.5.rest_6_
  54.2 0.2 collective-permute-start
  54.4 0.0 collective-permute-done.4.rest_5_
  54.4 0.7 %collective-permute-done.3.rest_4_ = bf16[64,256]{1,0:T(8,128)(2,1)S(1)} collective-permute-done((bf16[64,256]{1,0:T(8,128)(2,1)S(1)}, bf16[64,256]{1,0:T(8,128)(2,1)S(1)}, u32[]{:S(2)}, u32[]{:S(2)}) %collective-permute-start.3) | collective-permute-done | bytes 32800 | tf_op jit(solution)/shard_map/ppermute | solution.py:260
  55.1 0.9 %collective-permute-done.2.rest_3_ = bf16[64,256]{1,0:T(8,128)(2,1)S(1)} collective-permute-done((bf16[64,256]{1,0:T(8,128)(2,1)S(1)}, bf16[64,256]{1,0:T(8,128)(2,1)S(1)}, u32[]{:S(2)}, u32[]{:S(2)}) %collective-permute-start.2) | collective-permute-done | bytes 32800 | tf_op jit(solution)/shard_map/ppermute | solution.py:260
  55.9 1.6 %collective-permute-done.1.rest_2_ = bf16[64,256]{1,0:T(8,128)(2,1)S(1)} collective-permute-done((bf16[64,256]{1,0:T(8,128)(2,1)S(1)}, bf16[64,256]{1,0:T(8,128)(2,1)S(1)}, u32[]{:S(2)}, u32[]{:S(2)}) %collective-permute-start.1) | collective-permute-done | bytes 32800 | tf_op jit(solution)/shard_map/ppermute | solution.py:260
  57.5 0.0 collective-permute-done.rest_1_
  57.5 0.0 copy-done.1
  57.5 0.0 copy-done.6
  57.5 0.0 copy-done.3
  57.5 0.0 copy-done.2
  57.6 1.4 %last_sweep.1 = (f32[64,256]{1,0:T(8,128)}, f32[1,256]{1,0:T(1,128)}) custom-call(s32[1]{0:T(128)} %bitcast.me_ref, bf16[16,256,256]{2,1,0:T(8,128)(2,1)S(1)} %get-tuple-element.6.kernel_ref, bf16[64,256]{1,0:T(8,128)(2,1)S(1)} %get-tuple-element.7.rest_0_, bf16[64,256]{1,0:T(8,128)(2,1)S(1)} %collective-permute-done.rest_1_, ...), custom_call_target="tpu_custom_call" | custom-call | tf_op jit(solution)/shard_map/last_sweep/pallas_call | solution.py:261
Async XLA Ops:
  0.6 56.9 %copy-start.1 = (f32[64,256]{1,0:T(8,128)S(1)}, f32[64,256]{1,0:T(8,128)}, u32[]{:S(2)}) copy-start(f32[64,256]{1,0:T(8,128)} %rest_16_.1) | copy-start | bytes 196612
  0.6 56.9 %copy-start.6 = (f32[256]{0:T(256)S(1)}, f32[256]{0:T(256)}, u32[]{:S(2)}) copy-start(f32[256]{0:T(256)} %param.10) | copy-start | bytes 3076
  0.7 56.9 %copy-start.3 = (bf16[64,256]{1,0:T(8,128)(2,1)S(1)}, bf16[64,256]{1,0:T(8,128)(2,1)}, u32[]{:S(2)}) copy-start(bf16[64,256]{1,0:T(8,128)(2,1)} %rest_20_.1) | copy-start | bytes 98308
  0.7 56.9 %copy-start.2 = (bf16[64,256]{1,0:T(8,128)(2,1)S(1)}, bf16[64,256]{1,0:T(8,128)(2,1)}, u32[]{:S(2)}) copy-start(bf16[64,256]{1,0:T(8,128)(2,1)} %rest_19_.1) | copy-start | bytes 98308
  2.5 24.0 %all-to-all-start = ((bf16[16,80,256]{2,1,0:T(8,128)(2,1)}), bf16[16,80,256]{2,1,0:T(8,128)(2,1)S(1)}, u32[]{:S(2)}, u32[]{:S(2)}) async-start(bf16[16,80,256]{2,1,0:T(8,128)(2,1)} %prepare.1), calls=%async_computation | async-start | bytes 1310720 | tf_op jit(solution)/shard_map/all_to_all | solution.py:223
  26.4 0.8 %copy-start = (f32[64,256]{1,0:T(8,128)S(1)}, f32[64,256]{1,0:T(8,128)}, u32[]{:S(2)}) copy-start(f32[64,256]{1,0:T(8,128)} %rest_16_.1) | copy-start | bytes 196612
  27.3 0.7 %copy-start.4 = (f32[3,256]{1,0:T(4,128)S(1)}, f32[3,256]{1,0:T(4,128)}, u32[]{:S(2)}) copy-start(f32[3,256]{1,0:T(4,128)} %own_pos_ref.1) | copy-start | bytes 9220
  27.9 0.7 %copy-start.5 = (f32[256]{0:T(256)S(1)}, f32[256]{0:T(256)}, u32[]{:S(2)}) copy-start(f32[256]{0:T(256)} %param.10) | copy-start | bytes 3076
  28.6 0.7 %copy-start.7 = (f32[256]{0:T(256)S(1)}, f32[256]{0:T(256)}, u32[]{:S(2)}) copy-start(f32[256]{0:T(256)} %param.11) | copy-start | bytes 3076
  29.3 0.7 %copy-start.8 = (s32[2,32]{1,0:T(2,128)S(1)}, s32[2,32]{1,0:T(2,128)}, u32[]{:S(2)}) copy-start(s32[2,32]{1,0:T(2,128)} %words_ref.1) | copy-start | bytes 772
  33.8 8.1 %collective-permute-start.14 = (bf16[64,256]{1,0:T(8,128)(2,1)S(1)}, bf16[64,256]{1,0:T(8,128)(2,1)S(1)}, u32[]{:S(2)}, u32[]{:S(2)}) collective-permute-start(bf16[64,256]{1,0:T(8,128)(2,1)S(1)} %get-tuple-element.7.rest_0_), channel_id=1, source_target_pairs={{0,15},{1,14},{2,13},{3,12},{4,11},{5,10},{6,9},{7,8},{8,7},{9,6},... | collective-permute-start | bytes 98312 | tf_op jit(solution)/shard_map/ppermute | solution.py:260
  37.2 8.2 %collective-permute-start.13 = (bf16[64,256]{1,0:T(8,128)(2,1)S(1)}, bf16[64,256]{1,0:T(8,128)(2,1)S(1)}, u32[]{:S(2)}, u32[]{:S(2)}) collective-permute-start(bf16[64,256]{1,0:T(8,128)(2,1)S(1)} %get-tuple-element.7.rest_0_), channel_id=1, source_target_pairs={{0,14},{1,15},{2,12},{3,13},{4,10},{5,11},{6,8},{7,9},{8,6},{9,7},... | collective-permute-start | bytes 98312 | tf_op jit(solution)/shard_map/ppermute | solution.py:260
  38.3 7.1 %collective-permute-start.12 = (bf16[64,256]{1,0:T(8,128)(2,1)S(1)}, bf16[64,256]{1,0:T(8,128)(2,1)S(1)}, u32[]{:S(2)}, u32[]{:S(2)}) collective-permute-start(bf16[64,256]{1,0:T(8,128)(2,1)S(1)} %get-tuple-element.7.rest_0_), channel_id=1, source_target_pairs={{0,13},{1,12},{2,15},{3,14},{4,9},{5,8},{6,11},{7,10},{8,5},{9,4},... | collective-permute-start | bytes 98312 | tf_op jit(solution)/shard_map/ppermute | solution.py:260
  39.7 8.4 %collective-permute-start.11 = (bf16[64,256]{1,0:T(8,128)(2,1)S(1)}, bf16[64,256]{1,0:T(8,128)(2,1)S(1)}, u32[]{:S(2)}, u32[]{:S(2)}) collective-permute-start(bf16[64,256]{1,0:T(8,128)(2,1)S(1)} %get-tuple-element.7.rest_0_), channel_id=1, source_target_pairs={{0,12},{1,13},{2,14},{3,15},{4,8},{5,9},{6,10},{7,11},{8,4},{9,5},... | collective-permute-start | bytes 98312 | tf_op jit(solution)/shard_map/ppermute | solution.py:260
  41.9 7.5 %collective-permute-start.10 = (bf16[64,256]{1,0:T(8,128)(2,1)S(1)}, bf16[64,256]{1,0:T(8,128)(2,1)S(1)}, u32[]{:S(2)}, u32[]{:S(2)}) collective-permute-start(bf16[64,256]{1,0:T(8,128)(2,1)S(1)} %get-tuple-element.7.rest_0_), channel_id=1, source_target_pairs={{0,11},{1,10},{2,9},{3,8},{4,15},{5,14},{6,13},{7,12},{8,3},{9,2},... | collective-permute-start | bytes 98312 | tf_op jit(solution)/shard_map/ppermute | solution.py:260
  41.9 8.8 %collective-permute-start.9 = (bf16[64,256]{1,0:T(8,128)(2,1)S(1)}, bf16[64,256]{1,0:T(8,128)(2,1)S(1)}, u32[]{:S(2)}, u32[]{:S(2)}) collective-permute-start(bf16[64,256]{1,0:T(8,128)(2,1)S(1)} %get-tuple-element.7.rest_0_), channel_id=1, source_target_pairs={{0,10},{1,11},{2,8},{3,9},{4,14},{5,15},{6,12},{7,13},{8,2},{9,3},... | collective-permute-start | bytes 98312 | tf_op jit(solution)/shard_map/ppermute | solution.py:260
  45.4 5.5 %collective-permute-start.8 = (bf16[64,256]{1,0:T(8,128)(2,1)S(1)}, bf16[64,256]{1,0:T(8,128)(2,1)S(1)}, u32[]{:S(2)}, u32[]{:S(2)}) collective-permute-start(bf16[64,256]{1,0:T(8,128)(2,1)S(1)} %get-tuple-element.7.rest_0_), channel_id=1, source_target_pairs={{0,9},{1,8},{2,11},{3,10},{4,13},{5,12},{6,15},{7,14},{8,1},{9,0},... | collective-permute-start | bytes 98312 | tf_op jit(solution)/shard_map/ppermute | solution.py:260
  45.4 7.1 %collective-permute-start.7 = (bf16[64,256]{1,0:T(8,128)(2,1)S(1)}, bf16[64,256]{1,0:T(8,128)(2,1)S(1)}, u32[]{:S(2)}, u32[]{:S(2)}) collective-permute-start(bf16[64,256]{1,0:T(8,128)(2,1)S(1)} %get-tuple-element.7.rest_0_), channel_id=1, source_target_pairs={{0,8},{1,9},{2,10},{3,11},{4,12},{5,13},{6,14},{7,15},{8,0},{9,1},... | collective-permute-start | bytes 98312 | tf_op jit(solution)/shard_map/ppermute | solution.py:260
  48.1 5.5 %collective-permute-start.6 = (bf16[64,256]{1,0:T(8,128)(2,1)S(1)}, bf16[64,256]{1,0:T(8,128)(2,1)S(1)}, u32[]{:S(2)}, u32[]{:S(2)}) collective-permute-start(bf16[64,256]{1,0:T(8,128)(2,1)S(1)} %get-tuple-element.7.rest_0_), channel_id=1, source_target_pairs={{0,7},{1,6},{2,5},{3,4},{4,3},{5,2},{6,1},{7,0},{8,15},{9,14},{10,... | collective-permute-start | bytes 98312 | tf_op jit(solution)/shard_map/ppermute | solution.py:260
  49.4 4.8 %collective-permute-start.5 = (bf16[64,256]{1,0:T(8,128)(2,1)S(1)}, bf16[64,256]{1,0:T(8,128)(2,1)S(1)}, u32[]{:S(2)}, u32[]{:S(2)}) collective-permute-start(bf16[64,256]{1,0:T(8,128)(2,1)S(1)} %get-tuple-element.7.rest_0_), channel_id=1, source_target_pairs={{0,6},{1,7},{2,4},{3,5},{4,2},{5,3},{6,0},{7,1},{8,14},{9,15},{10,... | collective-permute-start | bytes 98312 | tf_op jit(solution)/shard_map/ppermute | solution.py:260
  50.7 3.7 %collective-permute-start.4 = (bf16[64,256]{1,0:T(8,128)(2,1)S(1)}, bf16[64,256]{1,0:T(8,128)(2,1)S(1)}, u32[]{:S(2)}, u32[]{:S(2)}) collective-permute-start(bf16[64,256]{1,0:T(8,128)(2,1)S(1)} %get-tuple-element.7.rest_0_), channel_id=1, source_target_pairs={{0,5},{1,4},{2,7},{3,6},{4,1},{5,0},{6,3},{7,2},{8,13},{9,12},{10,... | collective-permute-start | bytes 98312 | tf_op jit(solution)/shard_map/ppermute | solution.py:260
  50.9 4.2 %collective-permute-start.3 = (bf16[64,256]{1,0:T(8,128)(2,1)S(1)}, bf16[64,256]{1,0:T(8,128)(2,1)S(1)}, u32[]{:S(2)}, u32[]{:S(2)}) collective-permute-start(bf16[64,256]{1,0:T(8,128)(2,1)S(1)} %get-tuple-element.7.rest_0_), channel_id=1, source_target_pairs={{0,4},{1,5},{2,6},{3,7},{4,0},{5,1},{6,2},{7,3},{8,12},{9,13},{10,... | collective-permute-start | bytes 98312 | tf_op jit(solution)/shard_map/ppermute | solution.py:260
  52.5 3.4 %collective-permute-start.2 = (bf16[64,256]{1,0:T(8,128)(2,1)S(1)}, bf16[64,256]{1,0:T(8,128)(2,1)S(1)}, u32[]{:S(2)}, u32[]{:S(2)}) collective-permute-start(bf16[64,256]{1,0:T(8,128)(2,1)S(1)} %get-tuple-element.7.rest_0_), channel_id=1, source_target_pairs={{0,3},{1,2},{2,1},{3,0},{4,7},{5,6},{6,5},{7,4},{8,11},{9,10},{10,... | collective-permute-start | bytes 98312 | tf_op jit(solution)/shard_map/ppermute | solution.py:260
  53.6 3.9 %collective-permute-start.1 = (bf16[64,256]{1,0:T(8,128)(2,1)S(1)}, bf16[64,256]{1,0:T(8,128)(2,1)S(1)}, u32[]{:S(2)}, u32[]{:S(2)}) collective-permute-start(bf16[64,256]{1,0:T(8,128)(2,1)S(1)} %get-tuple-element.7.rest_0_), channel_id=1, source_target_pairs={{0,2},{1,3},{2,0},{3,1},{4,6},{5,7},{6,4},{7,5},{8,10},{9,11},{10,... | collective-permute-start | bytes 98312 | tf_op jit(solution)/shard_map/ppermute | solution.py:260
  54.2 3.3 %collective-permute-start = (bf16[64,256]{1,0:T(8,128)(2,1)S(1)}, bf16[64,256]{1,0:T(8,128)(2,1)S(1)}, u32[]{:S(2)}, u32[]{:S(2)}) collective-permute-start(bf16[64,256]{1,0:T(8,128)(2,1)S(1)} %get-tuple-element.7.rest_0_), channel_id=1, source_target_pairs={{0,1},{1,0},{2,3},{3,2},{4,5},{5,4},{6,7},{7,6},{8,9},{9,8},{10,11... | collective-permute-start | bytes 98312 | tf_op jit(solution)/shard_map/ppermute | solution.py:260
where the time goes:
time: 59.4 us; the launch traced here: 59 us
  starting transfers between devices  27.9 us (47%)
  waiting for transfers between devices  19.8 us (33%)
  Pallas kernels  7.02 us (12%)
  local copies, waits for them, and re-layouts  3.58 us (6%)
  between operations  0.72 us (1%)
    ppermute x15, starting transfers between devices, on_device(): pieces.append(lax.ppermute(scaled, 'row', pairs))  20.5 us
    all_to_all x1, waiting for transfers between devices, on_device(): packed = lax.all_to_all(packed, 'row', 0, 0)  16.6 us
    all_to_all x1, starting transfers between devices, on_device(): packed = lax.all_to_all(packed, 'row', 0, 0)  7.36 us
    pallas_call x1, Pallas kernels, on_device(): pl.pallas_call(functools.partial(first_sweep, scale), grid=(devices // ch...  3.82 us
    unnamed x18, local copies, waits for them, and re-layouts  3.58 us
    ppermute x15, waiting for transfers between devices, on_device(): pieces.append(lax.ppermute(scaled, 'row', pairs))  3.19 us
    pallas_call x1, Pallas kernels, on_device(): pl.pallas_call(prepare, in_specs=[vmem] * 3, out_specs=vmem, out_shape=ja...  1.78 us
    pallas_call x1, Pallas kernels, on_device(): pl.pallas_call(functools.partial(last_sweep_direct, scale, devices), in_s...  1.41 us
  transfers between devices with their start and end apart: 16, of which 4 were waited for; matrix products, arithmetic and copies ran while one was open for 0% of the time, Pallas kernels for 0%

commit v1 on v0

--- a/solution.py
+++ b/solution.py
@@ -12,7 +12,7 @@
 SWEEPS = 2
 GROUP = 16
 EXTRA = 16
-DIRECT = 16
+LINE = 4
 VMEM_BYTES = 48 * 1024 * 1024
 
 
@@ -89,9 +89,8 @@
         rows[3 * term : 3 * term + 3, :] = value
     scaled = (reflectance_ref[...] * seed_ref[...]).astype(jnp.bfloat16)
     extra = rows[...].astype(jnp.bfloat16)
-    for copy in range(out_ref.shape[0]):
-        out_ref[copy, :rhs_count] = scaled
-        out_ref[copy, rhs_count:] = extra
+    out_ref[:rhs_count] = scaled
+    out_ref[rhs_count:] = extra
 
 
 def lines_of(extra):
@@ -102,8 +101,13 @@
     ]
 
 
+def gathered_at(device):
+    return device % LINE * LINE + device // LINE
+
+
 def first_sweep(
     scale,
+    two_level,
     me_ref,
     words_ref,
     own_pos_ref,
@@ -128,7 +132,8 @@
 
     def form(at, carry):
         lines = lines_of(packed_ref[at, rhs_count:])
-        form_part(me, step * chunk + at, at, words_ref, lines, spread, kernel_ref)
+        part = gathered_at(at) if two_level else step * chunk + at
+        form_part(me, part, at, words_ref, lines, spread, kernel_ref)
         return carry
 
     lax.fori_loop(0, chunk, form, 0)
@@ -136,7 +141,8 @@
     @pl.when((me >= step * chunk) & (me < (step + 1) * chunk))
     def _():
         lines = [own_pos_ref[coord : coord + 1, :] for coord in range(3)]
-        form_diagonal(me, me - step * chunk, words_ref, lines, spread, kernel_ref)
+        at = gathered_at(me) if two_level else me - step * chunk
+        form_diagonal(me, at, words_ref, lines, spread, kernel_ref)
 
     held = total[...]
     for at in range(chunk):
@@ -176,12 +182,28 @@
         finish(scale, total[...], *rest[:-1])
 
 
-def last_sweep_direct(scale, pieces, me_ref, kernel_ref, *rest):
-    me = me_ref[0]
-    held = times_transpose(rest[0][...], kernel_ref[me])
-    for step in range(1, pieces):
-        held += times_transpose(rest[step][...], kernel_ref[jnp.bitwise_xor(me, step)])
-    finish(scale, held, *rest[pieces:])
+def last_sweep_lines(scale, me_ref, kernel_ref, every_ref, *rest):
+    line = me_ref[0] // LINE
+    held = None
+    for at in range(LINE * LINE):
+        column = at // LINE % 2 * 2 + at // LINE // 2
+        place = column * LINE + (line + (LINE - at % LINE)) % LINE
+        term = times_transpose(every_ref[at], kernel_ref[place])
+        held = term if held is None else held + term
+    finish(scale, held, *rest)
+
+
+def line_groups(devices, stride, count=LINE):
+    span = stride * count
+    return [
+        [base + offset + stride * at for at in range(count)]
+        for base in range(0, devices, span)
+        for offset in range(stride)
+    ]
+
+
+def shift_in_line(device, step):
+    return (device + LINE * step) % (LINE * LINE)
 
 
 def whole(shape):
@@ -199,7 +221,7 @@
     local_blocks = own_width // TILE
     scale = 1.0 / math.sqrt(own_width * devices)
     chunk = math.gcd(devices, 16)
-    direct = devices <= DIRECT and devices & (devices - 1) == 0
+    two_level = devices == LINE * LINE
     area = area.reshape(1, own_width)
     reflectance = reflectance.reshape(1, own_width)
     smem = pl.BlockSpec(memory_space=pltpu.SMEM)
@@ -214,17 +236,22 @@
         in_specs=[vmem] * 3,
         out_specs=vmem,
         out_shape=jax.ShapeDtypeStruct(
-            (devices if direct else 1, packed_rows, own_width), jnp.bfloat16
+            (packed_rows, own_width), jnp.bfloat16
         ),
         scratch_shapes=[pltpu.VMEM((EXTRA, own_width), jnp.float32)],
         name="prepare",
     )(position, adjoint_seed, reflectance)
-    if direct:
-        packed = lax.all_to_all(packed, "row", 0, 0)
+    if two_level:
+        packed = lax.all_gather(
+            packed, "row", axis_index_groups=line_groups(devices, LINE)
+        )
+        packed = lax.all_gather(
+            packed, "row", axis_index_groups=line_groups(devices, 1), tiled=True
+        )
     else:
-        packed = lax.all_gather(packed[0], "row")
+        packed = lax.all_gather(packed, "row")
     kernel, scaled = pl.pallas_call(
-        functools.partial(first_sweep, scale),
+        functools.partial(first_sweep, scale, two_level),
         grid=(devices // chunk,),
         in_specs=[
             smem,
@@ -253,19 +280,24 @@
         jax.ShapeDtypeStruct((1, own_width), jnp.float32),
     ]
     own = (adjoint_seed, area, reflectance, radiosity, emission)
-    if direct:
+    if two_level:
         pieces = [scaled]
-        for step in range(1, devices):
-            pairs = [(device, device ^ step) for device in range(devices)]
+        for step in range(1, LINE):
+            pairs = [(device, shift_in_line(device, step)) for device in range(devices)]
             pieces.append(lax.ppermute(scaled, "row", pairs))
+        every = jnp.stack(pieces)
+        for stride in (2, 1):
+            every = lax.all_gather(
+                every, "row", axis_index_groups=line_groups(devices, stride, 2), tiled=True
+            )
         adjoint, grad = pl.pallas_call(
-            functools.partial(last_sweep_direct, scale, devices),
-            in_specs=[smem] + [vmem] * (devices + 6),
+            functools.partial(last_sweep_lines, scale),
+            in_specs=[smem] + [vmem] * 7,
             out_specs=[vmem, vmem],
             out_shape=out_shape,
             compiler_params=pltpu.CompilerParams(vmem_limit_bytes=VMEM_BYTES),
             name="last_sweep",
-        )(my_index, kernel, *pieces, *own)
+        )(my_index, kernel, every, *own)
         return adjoint, grad.reshape(own_width)
 
     every = lax.all_gather(scaled, "row")

time: 59.4 us -> 52 us (0.88)
  blocking collectives: 0 us -> 31 us
  starting transfers between devices: 27.9 us -> 4.5 us
  waiting for transfers between devices: 19.8 us -> 5.07 us
    all_gather x0 -> x4, blocking collectives: none -> 31 us  [the longest x1 15.3 us: on_device(): lax.all_gather(packed, 'row', axis_index_groups=line_groups(devices, LINE))]
    all_to_all x1 -> x0, waiting for transfers between devices: 16.6 us -> none  [on_device(): packed = lax.all_to_all(packed, 'row', 0, 0)]
    ppermute x15 -> x3, starting transfers between devices: 20.5 us -> 4.5 us  [on_device(): pieces.append(lax.ppermute(scaled, 'row', pairs))]
    all_to_all x1 -> x0, starting transfers between devices: 7.36 us -> none  [on_device(): packed = lax.all_to_all(packed, 'row', 0, 0)]
    ppermute x15 -> x3, waiting for transfers between devices: 3.19 us -> 5.07 us  [on_device(): pieces.append(lax.ppermute(scaled, 'row', pairs))]
  transfers between devices with their start and end apart: 16 -> 3, of which waited for: 4 -> 3; matrix products, arithmetic and copies ran while one was open for 0% -> 0% of each run, Pallas kernels for 0% -> 0%
where the time goes in v1:
time: 52 us; the launch traced here: 51.6 us
  blocking collectives  31 us (60%)
  Pallas kernels  6.73 us (13%)
  waiting for transfers between devices  5.07 us (10%)
  starting transfers between devices  4.5 us (9%)
  local copies, waits for them, and re-layouts  3.58 us (7%)
  between operations  0.69 us (1%)
    all_gather x1, blocking collectives, on_device(): lax.all_gather(packed, 'row', axis_index_groups=line_groups(devices, LINE))  15.3 us
    all_gather x1, blocking collectives, on_device(): lax.all_gather(packed, 'row', axis_index_groups=line_groups(devices, 1),...  7.87 us
    all_gather x2, blocking collectives, on_device(): lax.all_gather(every, 'row', axis_index_groups=line_groups(devices, strid...  7.81 us
    ppermute x3, waiting for transfers between devices, on_device(): pieces.append(lax.ppermute(scaled, 'row', pairs))  5.07 us
    ppermute x3, starting transfers between devices, on_device(): pieces.append(lax.ppermute(scaled, 'row', pairs))  4.5 us
    pallas_call x1, Pallas kernels, on_device(): pl.pallas_call(functools.partial(first_sweep, scale, two_level), grid=(de...  3.82 us
    unnamed x18, local copies, waits for them, and re-layouts  3.58 us
    pallas_call x1, Pallas kernels, on_device(): pl.pallas_call(prepare, in_specs=[vmem] * 3, out_specs=vmem, out_shape=ja...  1.51 us
  transfers between devices with their start and end apart: 3, of which 3 were waited for; matrix products, arithmetic and copies ran while one was open for 0% of the time, Pallas kernels for 0%

profile of v1, /device:TPU:0, one launch (start us, length us, event | category | flops | bytes accessed | tf_op | source)
XLA Modules:
  0.0 51.6 jit_solution(14686467066296157688)
XLA Ops:
  0.6 0.0 copy-start.1
  0.6 0.0 copy-start.6
  0.7 0.0 copy-start.3
  0.7 0.0 copy-start.2
  0.7 1.5 %prepare.1 = bf16[80,256]{1,0:T(8,128)(2,1)} custom-call(f32[3,256]{1,0:T(4,128)} %own_pos_ref.1, f32[64,256]{1,0:T(8,128)} %rest_0_.1, f32[1,256]{1,0:T(1,128)} %bitcast.10), custom_call_target="tpu_custom_call" | custom-call | tf_op jit(solution)/shard_map/prepare/pallas_call | solution.py:234
  2.2 15.3 %all-gather = bf16[320,256]{1,0:T(8,128)(2,1)S(1)} all-gather(bf16[80,256]{1,0:T(8,128)(2,1)} %prepare.1), channel_id=2, replica_groups={{0,4,8,12},{1,5,9,13},{2,6,10,14},{3,7,11,15},{16,20,24,28},{17,21,25,2..., dimensions={0}, use_global_device_ids=true | all-gather | bytes 204800 | tf_op jit(solution)/shard_map/all_gather | solution.py:245
  17.5 7.9 %all_gather.17.packed_ref = bf16[16,80,256]{2,1,0:T(8,128)(2,1)S(1)} all-gather(bf16[4,80,256]{2,1,0:T(8,128)(2,1)S(1)} %bitcast.15), channel_id=1, replica_groups={{0,1,2,3},{4,5,6,7},{8,9,10,11},{12,13,14,15},{16,17,18,19},{20,21,22,2..., dimensions={0}, use_global_device_ids=true | all-gather | bytes 819200 | tf_op jit(solution)/shard_map/all_gather | solution.py:248
  25.4 0.0 copy-start
  25.4 0.8 %copy-done = f32[64,256]{1,0:T(8,128)S(1)} copy-done((f32[64,256]{1,0:T(8,128)S(1)}, f32[64,256]{1,0:T(8,128)}, u32[]{:S(2)}) %copy-start) | copy-done | bytes 65560
  26.2 0.0 copy-start.4
  26.2 0.7 %copy-done.4 = f32[3,256]{1,0:T(4,128)S(1)} copy-done((f32[3,256]{1,0:T(4,128)S(1)}, f32[3,256]{1,0:T(4,128)}, u32[]{:S(2)}) %copy-start.4) | copy-done | bytes 3096
  26.9 0.0 copy-start.5
  26.9 0.7 %copy-done.5 = f32[256]{0:T(256)S(1)} copy-done((f32[256]{0:T(256)S(1)}, f32[256]{0:T(256)}, u32[]{:S(2)}) %copy-start.5) | copy-done | bytes 1048
  27.6 0.0 copy-start.7
  27.6 0.7 %copy-done.7 = f32[256]{0:T(256)S(1)} copy-done((f32[256]{0:T(256)S(1)}, f32[256]{0:T(256)}, u32[]{:S(2)}) %copy-start.7) | copy-done | bytes 1048
  28.3 0.0 copy-start.8
  28.3 0.7 %copy-done.8 = s32[2,32]{1,0:T(2,128)S(1)} copy-done((s32[2,32]{1,0:T(2,128)S(1)}, s32[2,32]{1,0:T(2,128)}, u32[]{:S(2)}) %copy-start.8) | copy-done | bytes 280
  29.0 3.8 %first_sweep.1 = (bf16[16,256,256]{2,1,0:T(8,128)(2,1)S(1)}, bf16[64,256]{1,0:T(8,128)(2,1)S(1)}) custom-call(s32[1]{0:T(128)} %bitcast.me_ref, s32[2,32]{1,0:T(2,128)S(1)} %copy-done.8, f32[3,256]{1,0:T(4,128)S(1)} %copy-done.4, bf16[16,80,256]{2,1,0:T(8,128)(2,1)S(1)} %all_gather.17.packed_ref, f32[64,256]{1,0:T(8,128)S(1)} %copy-done, ...), custom_call_target="tpu_custom_call" | custom-call | tf_op jit(solution)/shard_map/first_sweep/pallas_call | solution.py:253
  32.8 3.9 %collective-permute-start.2 = (bf16[64,256]{1,0:T(8,128)(2,1)S(1)}, bf16[64,256]{1,0:T(8,128)(2,1)S(1)}, u32[]{:S(2)}, u32[]{:S(2)}) collective-permute-start(bf16[64,256]{1,0:T(8,128)(2,1)S(1)} %get-tuple-element.7), channel_id=1, source_target_pairs={{0,12},{1,13},{2,14},{3,15},{4,0},{5,1},{6,2},{7,3},{8,4},{9,5},{1... | collective-permute-start | bytes 98312 | tf_op jit(solution)/shard_map/ppermute | solution.py:287
  36.7 0.0 collective-permute-start.1
  36.7 0.6 %collective-permute-start = (bf16[64,256]{1,0:T(8,128)(2,1)S(1)}, bf16[64,256]{1,0:T(8,128)(2,1)S(1)}, u32[]{:S(2)}, u32[]{:S(2)}) collective-permute-start(bf16[64,256]{1,0:T(8,128)(2,1)S(1)} %get-tuple-element.7), channel_id=1, source_target_pairs={{0,4},{1,5},{2,6},{3,7},{4,8},{5,9},{6,10},{7,11},{8,12},{9,13},{1... | collective-permute-start | bytes 98312 | tf_op jit(solution)/shard_map/ppermute | solution.py:287
  37.3 1.1 %collective-permute-done.2 = bf16[64,256]{1,0:T(8,128)(2,1)S(1)} collective-permute-done((bf16[64,256]{1,0:T(8,128)(2,1)S(1)}, bf16[64,256]{1,0:T(8,128)(2,1)S(1)}, u32[]{:S(2)}, u32[]{:S(2)}) %collective-permute-start.2) | collective-permute-done | bytes 32800 | tf_op jit(solution)/shard_map/ppermute | solution.py:287
  38.4 3.4 %collective-permute-done.1 = bf16[64,256]{1,0:T(8,128)(2,1)S(1)} collective-permute-done((bf16[64,256]{1,0:T(8,128)(2,1)S(1)}, bf16[64,256]{1,0:T(8,128)(2,1)S(1)}, u32[]{:S(2)}, u32[]{:S(2)}) %collective-permute-start.1) | collective-permute-done | bytes 32800 | tf_op jit(solution)/shard_map/ppermute | solution.py:287
  41.8 0.6 %collective-permute-done = bf16[64,256]{1,0:T(8,128)(2,1)S(1)} collective-permute-done((bf16[64,256]{1,0:T(8,128)(2,1)S(1)}, bf16[64,256]{1,0:T(8,128)(2,1)S(1)}, u32[]{:S(2)}, u32[]{:S(2)}) %collective-permute-start) | collective-permute-done | bytes 32800 | tf_op jit(solution)/shard_map/ppermute | solution.py:287
  42.4 5.6 %all_gather.18 = bf16[8,64,256]{2,1,0:T(8,128)(2,1)S(1)} all-gather(bf16[4,64,256]{2,1,0:T(8,128)(2,1)S(1)} %pad_maximum_fusion), channel_id=1, replica_groups={{0,2},{1,3},{4,6},{5,7},{8,10},{9,11},{12,14},{13,15},{16,18},{17,19},{..., dimensions={0}, use_global_device_ids=true | all-gather | bytes 393216 | tf_op jit(solution)/shard_map/all_gather | solution.py:290
  48.0 2.2 %all_gather.19.every_ref = bf16[16,64,256]{2,1,0:T(8,128)(2,1)S(1)} all-gather(bf16[8,64,256]{2,1,0:T(8,128)(2,1)S(1)} %all_gather.18), channel_id=1, replica_groups={{0,1},{2,3},{4,5},{6,7},{8,9},{10,11},{12,13},{14,15},{16,17},{18,19},{..., dimensions={0}, use_global_device_ids=true | all-gather | bytes 786432 | tf_op jit(solution)/shard_map/all_gather | solution.py:290
  50.2 0.0 copy-done.1
  50.2 0.0 copy-done.6
  50.2 0.0 copy-done.3
  50.2 0.0 copy-done.2
  50.2 1.4 %last_sweep.1 = (f32[64,256]{1,0:T(8,128)}, f32[1,256]{1,0:T(1,128)}) custom-call(s32[1]{0:T(128)} %bitcast.me_ref, bf16[16,256,256]{2,1,0:T(8,128)(2,1)S(1)} %get-tuple-element.6.kernel_ref, bf16[16,64,256]{2,1,0:T(8,128)(2,1)S(1)} %all_gather.19.every_ref, f32[64,256]{1,0:T(8,128)S(1)} %copy-done.1, f32[1,256]{1,0:T(1,128)S(1)} %bitcast.14, ...), custom_call_target="tpu_custom_call" | custom-call | tf_op jit(solution)/shard_map/last_sweep/pallas_call | solution.py:293
  (1 shorter events, 0.0 us)
Async XLA Ops:
  0.6 49.6 %copy-start.1 = (f32[64,256]{1,0:T(8,128)S(1)}, f32[64,256]{1,0:T(8,128)}, u32[]{:S(2)}) copy-start(f32[64,256]{1,0:T(8,128)} %rest_0_.1) | copy-start | bytes 196612
  0.6 49.6 %copy-start.6 = (f32[256]{0:T(256)S(1)}, f32[256]{0:T(256)}, u32[]{:S(2)}) copy-start(f32[256]{0:T(256)} %param.10) | copy-start | bytes 3076
  0.7 49.6 %copy-start.3 = (bf16[64,256]{1,0:T(8,128)(2,1)S(1)}, bf16[64,256]{1,0:T(8,128)(2,1)}, u32[]{:S(2)}) copy-start(bf16[64,256]{1,0:T(8,128)(2,1)} %rest_4_.1) | copy-start | bytes 98308
  0.7 49.6 %copy-start.2 = (bf16[64,256]{1,0:T(8,128)(2,1)S(1)}, bf16[64,256]{1,0:T(8,128)(2,1)}, u32[]{:S(2)}) copy-start(bf16[64,256]{1,0:T(8,128)(2,1)} %rest_3_.1) | copy-start | bytes 98308
  25.4 0.8 %copy-start = (f32[64,256]{1,0:T(8,128)S(1)}, f32[64,256]{1,0:T(8,128)}, u32[]{:S(2)}) copy-start(f32[64,256]{1,0:T(8,128)} %rest_0_.1) | copy-start | bytes 196612
  26.2 0.7 %copy-start.4 = (f32[3,256]{1,0:T(4,128)S(1)}, f32[3,256]{1,0:T(4,128)}, u32[]{:S(2)}) copy-start(f32[3,256]{1,0:T(4,128)} %own_pos_ref.1) | copy-start | bytes 9220
  26.9 0.7 %copy-start.5 = (f32[256]{0:T(256)S(1)}, f32[256]{0:T(256)}, u32[]{:S(2)}) copy-start(f32[256]{0:T(256)} %param.10) | copy-start | bytes 3076
  27.6 0.7 %copy-start.7 = (f32[256]{0:T(256)S(1)}, f32[256]{0:T(256)}, u32[]{:S(2)}) copy-start(f32[256]{0:T(256)} %param.11) | copy-start | bytes 3076
  28.3 0.7 %copy-start.8 = (s32[2,32]{1,0:T(2,128)S(1)}, s32[2,32]{1,0:T(2,128)}, u32[]{:S(2)}) copy-start(s32[2,32]{1,0:T(2,128)} %words_ref.1) | copy-start | bytes 772
  32.8 5.6 %collective-permute-start.2 = (bf16[64,256]{1,0:T(8,128)(2,1)S(1)}, bf16[64,256]{1,0:T(8,128)(2,1)S(1)}, u32[]{:S(2)}, u32[]{:S(2)}) collective-permute-start(bf16[64,256]{1,0:T(8,128)(2,1)S(1)} %get-tuple-element.7), channel_id=1, source_target_pairs={{0,12},{1,13},{2,14},{3,15},{4,0},{5,1},{6,2},{7,3},{8,4},{9,5},{1... | collective-permute-start | bytes 98312 | tf_op jit(solution)/shard_map/ppermute | solution.py:287
  36.7 5.2 %collective-permute-start.1 = (bf16[64,256]{1,0:T(8,128)(2,1)S(1)}, bf16[64,256]{1,0:T(8,128)(2,1)S(1)}, u32[]{:S(2)}, u32[]{:S(2)}) collective-permute-start(bf16[64,256]{1,0:T(8,128)(2,1)S(1)} %get-tuple-element.7), channel_id=1, source_target_pairs={{0,8},{1,9},{2,10},{3,11},{4,12},{5,13},{6,14},{7,15},{8,0},{9,1},... | collective-permute-start | bytes 98312 | tf_op jit(solution)/shard_map/ppermute | solution.py:287
  36.7 5.7 %collective-permute-start = (bf16[64,256]{1,0:T(8,128)(2,1)S(1)}, bf16[64,256]{1,0:T(8,128)(2,1)S(1)}, u32[]{:S(2)}, u32[]{:S(2)}) collective-permute-start(bf16[64,256]{1,0:T(8,128)(2,1)S(1)} %get-tuple-element.7), channel_id=1, source_target_pairs={{0,4},{1,5},{2,6},{3,7},{4,8},{5,9},{6,10},{7,11},{8,12},{9,13},{1... | collective-permute-start | bytes 98312 | tf_op jit(solution)/shard_map/ppermute | solution.py:287
